TPU v7x, 256 devices: a whole 4x4x8 slice. The times are simulated.
256 devices in a mesh: scene: 8 (over y, core), blk: 32 (over x, z).
Axes of the slice: x: 4, y: 4, z: 8, core: 2. Of those that a mesh axis runs over, the one named last changes fastest.
Arguments:
- coarse_feat: bfloat16 [8, 128, 64, 256], P('scene', 'blk'), may hold values from -6 to 6
- coarse_nbr: int32 [8, 128, 4], P('scene', 'blk'), may hold values from -1 to 127, as said below
- fine_dest: int32 [8, 128], P('scene', 'blk'), may hold values from 0 to 127, as said below
- fine_nbr: int32 [8, 128, 4], P('scene', 'blk'), may hold values from -1 to 127, as said below
- skip: bfloat16 [8, 128, 512, 128], P('scene', 'blk'), may hold values from -12 to 12
- cotangent: bfloat16 [8, 128, 512, 128], P('scene', 'blk'), may hold values from -0.0078125 to 0.0078125
- w_coarse: bfloat16 [27, 256, 256], replicated, may hold values from -0.078125 to 0.078125
- w_up: bfloat16 [256, 128], replicated, may hold values from -0.375 to 0.375
- w_fine: bfloat16 [27, 128, 128], replicated, may hold values from -0.109375 to 0.109375
Outputs:
- fine_out: bfloat16 [8, 128, 512, 128], P('scene', 'blk')
- grad_fine: float32 [128, 27, 128], P('blk')
Inputs may be any that keep to these rules, and one draw needn't show every extreme that they name: `coarse_nbr`: entry k of coarse block b is the coarse index of the block beside b's face k, or -1. Neighbours are mutual, and lie on b's own device along blk or on the device just before or after it. `fine_dest`: for each scene a permutation of 0 to 127. Of the blocks that one device along blk holds in coarse order, at most 1 go to any one device along blk in fine order (fine index // 4), and that many do for some pair of devices. Entry k of fine block f is the fine index of the block beside f's face k, or -1; fine_nbr[s, fine_dest[s, b], k] = fine_dest[s, coarse_nbr[s, b, k]] where that entry is not -1, else -1. Neighbours lie on f's own device along blk or on the device just before or after it.
All inputs are finite; a program needn't handle non-finite values.
Results may differ from a plain program's by a relative error of at most 0.0058.
Values may be sent and summed in bfloat16 or wider, within the bound.
A program may use at most 64 MiB of HBM per device.

v0:
```python
import jax
import jax.numpy as jnp
from jax import lax
from jax.sharding import PartitionSpec as P

CEDGE = 4
FEDGE = 8


def with_halo(cells, sides, width):
    for axis, dim in sides:
        count = lax.axis_size(axis)
        ends = count - 1
        head = lax.slice_in_dim(cells, 0, width, axis=dim)
        tail = lax.slice_in_dim(cells, cells.shape[dim] - width, cells.shape[dim], axis=dim)
        cells = jnp.concatenate(
            [
                lax.ppermute(tail, axis, [(i, (i + 1) % count) for i in range(ends)]),
                cells,
                lax.ppermute(head, axis, [((i + 1) % count, i) for i in range(ends)]),
            ],
            axis=dim,
        )
    return cells


def upsample(block_cells, side_cells):
    block_count = block_cells.shape[0]
    channels = block_cells.shape[-1]
    cell_grid = block_cells.reshape(block_count, side_cells, side_cells, side_cells, channels)
    cell_grid = jnp.repeat(jnp.repeat(jnp.repeat(cell_grid, 2, axis=1), 2, axis=2), 2, axis=3)
    return cell_grid.reshape(block_count, 8 * side_cells**3, channels)


def facing_layers(cell_grid):
    return jnp.stack(
        [cell_grid[:, -1], cell_grid[:, 0], cell_grid[:, :, -1], cell_grid[:, :, 0]], axis=1
    )


def pad_faces(cell_grid, layers):
    padded = jnp.pad(cell_grid, ((0, 0), (1, 1), (1, 1), (1, 1), (0, 0)))
    padded = padded.at[:, 0, 1:-1, 1:-1].set(layers[:, 0])
    padded = padded.at[:, -1, 1:-1, 1:-1].set(layers[:, 1])
    padded = padded.at[:, 1:-1, 0, 1:-1].set(layers[:, 2])
    padded = padded.at[:, 1:-1, -1, 1:-1].set(layers[:, 3])
    return padded


def neighbour_layers(extended, face_table, first_index):
    row_count = extended.shape[0]
    block_count = face_table.shape[0]
    relative = face_table - first_index
    positions = jnp.arange(row_count, dtype=jnp.int32)
    chosen = []
    for face_index in range(4):
        selector = (
            (relative[:, face_index][:, None] == positions[None, :])
            & (face_table[:, face_index][:, None] >= 0)
        ).astype(jnp.bfloat16)
        flattened = extended[:, face_index].reshape(row_count, -1)
        fetched = jnp.dot(selector, flattened, preferred_element_type=jnp.float32).astype(
            jnp.bfloat16
        )
        chosen.append(fetched.reshape((block_count,) + extended.shape[2:]))
    return jnp.stack(chosen, axis=1)


def convolve(padded, weight, side_cells):
    block_count = padded.shape[0]
    channels = padded.shape[-1]
    running = None
    for off_x in range(3):
        for off_y in range(3):
            stacked = jnp.concatenate(
                [
                    padded[
                        :,
                        off_x : off_x + side_cells,
                        off_y : off_y + side_cells,
                        off_z : off_z + side_cells,
                    ]
                    for off_z in range(3)
                ],
                axis=-1,
            ).reshape(block_count * side_cells**3, 3 * channels)
            first_tap = 9 * off_x + 3 * off_y
            product = jnp.dot(
                stacked,
                weight[first_tap : first_tap + 3].reshape(3 * channels, -1),
                preferred_element_type=jnp.float32,
            )
            running = product if running is None else running + product
    return running


def silu_slope(pre_value):
    sigmoid_value = jax.nn.sigmoid(pre_value)
    return sigmoid_value * (1.0 + pre_value * (1.0 - sigmoid_value))


def body(coarse_feat, coarse_nbr, fine_dest, fine_nbr, skip, cotangent, w_coarse, w_up, w_fine):
    blocks = coarse_feat.shape[1]
    fine_chans = w_fine.shape[-1]
    peer_count = lax.axis_size("blk")
    repeats = (blocks + peer_count - 1) // peer_count
    position = lax.axis_index("blk")
    first_index = (position - 1) * blocks
    own_blocks = position * blocks + jnp.arange(blocks, dtype=jnp.int32)
    slot_index = jnp.arange(peer_count * repeats, dtype=jnp.int32)
    earlier = (
        jnp.arange(blocks, dtype=jnp.int32)[:, None] < jnp.arange(blocks, dtype=jnp.int32)[None, :]
    )
    coarse_grid = coarse_feat[0].reshape(blocks, CEDGE, CEDGE, CEDGE, -1)
    coarse_ext = with_halo(facing_layers(coarse_grid), (("blk", 0),), blocks)
    coarse_padded = pad_faces(coarse_grid, neighbour_layers(coarse_ext, coarse_nbr[0], first_index))
    coarse_act = jax.nn.silu(convolve(coarse_padded, w_coarse, CEDGE)).astype(jnp.bfloat16)
    projected = jnp.dot(coarse_act, w_up, preferred_element_type=jnp.float32).astype(jnp.bfloat16)
    projected = projected.reshape(blocks, CEDGE**3, fine_chans)
    target = fine_dest[0]
    owners = target // blocks
    same_owner = owners[:, None] == owners[None, :]
    rank = jnp.sum((same_owner & earlier).astype(jnp.int32), axis=0)
    slot_of = owners * repeats + rank
    to_slot = slot_of[None, :] == slot_index[:, None]
    labels = jnp.max(jnp.where(to_slot, target[None, :], -1), axis=1)
    weights_send = to_slot.astype(jnp.bfloat16)
    packed = jnp.dot(
        weights_send,
        upsample(projected, CEDGE).reshape(blocks, -1),
        preferred_element_type=jnp.float32,
    ).astype(jnp.bfloat16)
    arrived = lax.all_to_all(packed, "blk", split_axis=0, concat_axis=0, tiled=True)
    sources = lax.all_to_all(labels, "blk", split_axis=0, concat_axis=0, tiled=True)
    matches = (sources[None, :] == own_blocks[:, None]).astype(jnp.bfloat16)
    placed = jnp.dot(matches, arrived, preferred_element_type=jnp.float32).astype(jnp.bfloat16)
    fine_up = placed.reshape(blocks, FEDGE**3, fine_chans)
    hidden = (fine_up.astype(jnp.float32) + skip[0].astype(jnp.float32)).astype(jnp.bfloat16)
    fine_grid = hidden.reshape(blocks, FEDGE, FEDGE, FEDGE, fine_chans)
    fine_ext = with_halo(facing_layers(fine_grid), (("blk", 0),), blocks)
    fine_padded = pad_faces(fine_grid, neighbour_layers(fine_ext, fine_nbr[0], first_index))
    pre_fine = convolve(fine_padded, w_fine, FEDGE)
    outputs = [jax.nn.silu(pre_fine).astype(jnp.bfloat16).reshape(blocks, FEDGE**3, fine_chans)]
    delta_fine = (
        cotangent[0].reshape(-1, fine_chans).astype(jnp.float32) * silu_slope(pre_fine)
    ).astype(jnp.bfloat16)
    fine_out = jnp.stack(outputs)
    shard_rows = fine_chans // peer_count
    fine_padded, delta_fine = (fine_padded, delta_fine)
    tap_terms = []
    for off_x in range(3):
        for off_y in range(3):
            for off_z in range(3):
                piece = fine_padded[
                    :, off_x : off_x + FEDGE, off_y : off_y + FEDGE, off_z : off_z + FEDGE
                ].reshape(-1, fine_chans)
                tap_terms.append(
                    lax.dot_general(
                        piece,
                        delta_fine,
                        (((0,), (0,)), ((), ())),
                        preferred_element_type=jnp.float32,
                    )
                )
    running = jnp.stack(tap_terms, axis=1)
    summed = lax.psum(running, ("scene", "blk"))
    gradient = lax.dynamic_slice_in_dim(summed, position * shard_rows, shard_rows, 0)
    return (fine_out, gradient)


def solution(mesh):
    in_specs = (
        P("scene", "blk", None, None),
        P("scene", "blk", None),
        P("scene", "blk"),
        P("scene", "blk", None),
        P("scene", "blk", None, None),
        P("scene", "blk", None, None),
        P(),
        P(),
        P(),
    )
    out_specs = (P("scene", "blk", None, None), P("blk", None, None))
    return jax.shard_map(body, mesh=mesh, in_specs=in_specs, out_specs=out_specs, check_vma=False)
```

profile of v0, /device:TPU:2, one launch (start us, length us, event | category | flops | bytes accessed | tf_op | source)
XLA Modules:
  0.0 550.9 jit_solution(13759486911065288850)
XLA Ops:
  7.2 1.0 reshape_squeeze.28
  9.6 7.7 %collective-permute-start.1 = (bf16[4,4,4,4,256]{4,3,2,0,1:T(4,128)(2,1)}, bf16[4,4,4,4,256]{4,3,2,0,1:T(4,128)(2,1)}, u32[]{:S(2)}, u32[]{:S(2)}) collective-permute-start(bf16[4,4,4,4,256]{4,3,2,0,1:T(4,128)(2,1)} %pad_maximum_fusion.21), channel_id=1, source_target_pairs={{1,0},{2,1},{3,2},{4,3},{5,4},{6,5},{7,6},{8,7},{9,8},{10,9},{11,1... | collective-permute-start | bytes 393224 | tf_op jit(solution)/shard_map/ppermute | solution.py:20
  17.3 1.9 collective-permute-start
  23.4 8.6 %all-to-all-start = ((s32[32,1,1]{2,1,0:T(1,128)}), s32[32,1,1]{2,1,0:T(1,128)S(1)}, u32[]{:S(2)}, u32[]{:S(2)}) async-start(s32[32,1,1]{2,1,0:T(1,128)} %copy.71), calls=%async_computation | async-start | bytes 32768 | tf_op jit(solution)/shard_map/all_to_all | solution.py:134
  32.0 3.1 fusion.88
  36.5 1.6 fusion.53
  38.2 1.4 pad_maximum_fusion.10
  39.6 0.8 fusion.95
  40.4 1.6 reshape_squeeze.29
  42.0 1.7 convolution_convert_fusion.9
  43.7 0.8 reshape.605
  44.5 1.6 reshape_squeeze.30
  46.1 1.7 convolution_convert_fusion.8
  47.8 1.4 reshape.606
  49.3 1.6 reshape_squeeze.31
  50.8 1.7 convolution_convert_fusion.7
  52.6 1.4 reshape.607
  54.7 1.1 convolution_convert_fusion.6
  56.1 0.9 scatter.29
  57.0 0.9 scatter.30
  58.6 1.1 fusion.94
  59.8 2.3 fusion.93
  62.3 0.8 reshape.609
  63.1 1.2 pad_maximum_fusion.12
  64.3 0.8 reshape.611
  65.1 1.1 pad_maximum_fusion.13
  66.3 0.9 reshape.613
  67.2 1.2 pad_maximum_fusion.14
  68.4 0.8 reshape.615
  69.2 1.2 pad_maximum_fusion.15
  70.4 0.9 reshape.617
  71.3 1.1 pad_maximum_fusion.16
  72.5 0.8 reshape.619
  73.3 1.2 pad_maximum_fusion.17
  74.5 0.9 reshape.621
  75.4 2.0 pad_maximum_fusion.18
  77.4 1.8 reshape.623
  79.3 1.8 pad_maximum_fusion.19
  81.1 1.8 reshape.625
  82.9 1.3 fusion.96
  84.3 1.3 convolution_add_fusion.15
  89.0 3.3 fusion
  92.9 6.8 %reduce.49 = bf16[32,65536]{1,0:T(8,128)(2,1)} reduce(bf16[32,1,65536]{2,0,1:T(8,128)(2,1)} %fusion, bf16[]{:T(256)} %broadcast.212), dimensions={1}, to_apply=%copy.79.reduce_sub_computation | reduce | bytes 8388610 | tf_op jit(solution)/shard_map/all_to_all | solution.py:133
  99.7 6.6 %reshape.698 = bf16[32,2,32768]{2,1,0:T(2,128)(2,1)} reshape(bf16[32,65536]{1,0:T(8,128)(2,1)} %reduce.49) | data formatting | bytes 8388608
  106.2 10.0 %all-to-all-start.1 = ((bf16[32,2,32768]{2,1,0:T(2,128)(2,1)}), bf16[32,2,32768]{2,1,0:T(2,128)(2,1)}, u32[]{:S(2)}, u32[]{:S(2)}) async-start(bf16[32,2,32768]{2,1,0:T(2,128)(2,1)} %reshape.698), calls=%async_computation.1 | async-start | bytes 8388608 | tf_op jit(solution)/shard_map/all_to_all | solution.py:133
  117.7 91.8 %all-to-all-done.1 = bf16[32,2,32768]{2,1,0:T(2,128)(2,1)} async-done(((bf16[32,2,32768]{2,1,0:T(2,128)(2,1)}), bf16[32,2,32768]{2,1,0:T(2,128)(2,1)}, u32[]{:S(2)}, u32[]{:S(2)}) %all-to-all-start.1) | async-done | bytes 4194336 | tf_op jit(solution)/shard_map/all_to_all | solution.py:133
  209.5 20.0 %reshape.699 = bf16[32,1,65536]{2,1,0:T(2,128)(2,1)} reshape(bf16[32,2,32768]{2,1,0:T(2,128)(2,1)} %all-to-all-done.1) | data formatting | bytes 8388608
  229.5 7.9 %fusion.4 = f32[1,4,512,128]{3,1,2,0:T(4,128)S(1)} fusion(bf16[32,1,65536]{2,1,0:T(2,128)(2,1)} %reshape.699, s32[32]{0:T(128)S(1)} %reduce.16, s32[4]{0:T(128)S(1)} %iota_add_fusion), kind=kOutput, calls=%fused_computation.31 | convolution fusion | flops 17301632 | bytes 5243024 | tf_op jit(solution)/shard_map/dot_general | solution.py:136
  237.6 0.9 copy-done.14
  238.8 4.4 collective-permute-start.3
  243.2 2.0 collective-permute-start.2
  245.2 0.8 slice_reduce_fusion
  247.1 2.2 collective-permute-done.3
  249.3 5.8 %collective-permute-done.2 = bf16[4,4,8,8,128]{4,3,2,0,1:T(8,128)(2,1)S(1)} collective-permute-done((bf16[4,4,8,8,128]{4,3,2,0,1:T(8,128)(2,1)S(1)}, bf16[4,4,8,8,128]{4,3,2,0,1:T(8,128)(2,1)S(1)}, u32[]{:S(2)}, u32[]{:S(2)}) %collective-permute-start.2) | collective-permute-done | bytes 262176 | tf_op jit(solution)/shard_map/ppermute | solution.py:18
  255.5 0.9 fusion.7
  256.6 0.9 fusion.8
  257.6 0.8 fusion.9
  258.6 0.9 fusion.10
  260.5 0.9 fusion.90
  261.4 2.8 fusion.89
  271.9 1.7 fusion.38
  283.2 1.2 copy-done.2
  284.4 257.9 %all-reduce.4.cloned.1.call-done = f32[128,27,128]{2,0,1:T(8,128)} async-done(((f32[128,27,128]{2,0,1:T(8,128)}), f32[128,27,128]{2,0,1:T(8,128)}) %all-reduce.4.cloned.1.call-update) | async-done | bytes 1769488 | tf_op jit(solution)/shard_map/psum | solution.py:166
  542.3 1.5 constant_dynamic-slice_fusion
  (168 shorter events, 34.1 us)
Async XLA Ops:
  7.2 80.4 %copy-start = (bf16[256,128]{1,0:T(8,128)(2,1)S(1)}, bf16[256,128]{1,0:T(8,128)(2,1)}, u32[]{:S(2)}) copy-start(bf16[256,128]{1,0:T(8,128)(2,1)} %param.32) | copy-start | bytes 196612
  8.2 0.6 copy-start.17
  8.2 1.4 copy-start.18
  8.2 9.1 %copy-start.19 = (bf16[4,1,4,4,256]{4,3,2,0,1:T(4,128)(2,1)}, bf16[4,1,4,4,256]{4,3,2,0,1:T(4,128)(2,1)S(1)}, u32[]{:S(2)}) copy-start(bf16[4,1,4,4,256]{4,3,2,0,1:T(4,128)(2,1)S(1)} %get-tuple-element.200) | copy-start | bytes 98308
  8.3 11.0 %copy-start.20 = (bf16[4,1,4,4,256]{4,3,2,0,1:T(4,128)(2,1)}, bf16[4,1,4,4,256]{4,3,2,0,1:T(4,128)(2,1)S(1)}, u32[]{:S(2)}) copy-start(bf16[4,1,4,4,256]{4,3,2,0,1:T(4,128)(2,1)S(1)} %get-tuple-element.201) | copy-start | bytes 98308
  9.6 28.6 %collective-permute-start.1 = (bf16[4,4,4,4,256]{4,3,2,0,1:T(4,128)(2,1)}, bf16[4,4,4,4,256]{4,3,2,0,1:T(4,128)(2,1)}, u32[]{:S(2)}, u32[]{:S(2)}) collective-permute-start(bf16[4,4,4,4,256]{4,3,2,0,1:T(4,128)(2,1)} %pad_maximum_fusion.21), channel_id=1, source_target_pairs={{1,0},{2,1},{3,2},{4,3},{5,4},{6,5},{7,6},{8,7},{9,8},{10,9},{11,1... | collective-permute-start | bytes 393224 | tf_op jit(solution)/shard_map/ppermute | solution.py:20
  17.3 20.9 %collective-permute-start = (bf16[4,4,4,4,256]{4,3,2,0,1:T(4,128)(2,1)}, bf16[4,4,4,4,256]{4,3,2,0,1:T(4,128)(2,1)}, u32[]{:S(2)}, u32[]{:S(2)}) collective-permute-start(bf16[4,4,4,4,256]{4,3,2,0,1:T(4,128)(2,1)} %pad_maximum_fusion.21), channel_id=1, source_target_pairs={{0,1},{1,2},{2,3},{3,4},{4,5},{5,6},{6,7},{7,8},{8,9},{9,10},{10,1... | collective-permute-start | bytes 393224 | tf_op jit(solution)/shard_map/ppermute | solution.py:18
  21.3 0.6 copy-start.30
  23.4 82.9 %all-to-all-start = ((s32[32,1,1]{2,1,0:T(1,128)}), s32[32,1,1]{2,1,0:T(1,128)S(1)}, u32[]{:S(2)}, u32[]{:S(2)}) async-start(s32[32,1,1]{2,1,0:T(1,128)} %copy.71), calls=%async_computation | async-start | bytes 32768 | tf_op jit(solution)/shard_map/all_to_all | solution.py:134
  32.0 3.1 copy-start.22
  32.0 3.1 copy-start.23
  36.5 5.5 copy-start.32
  62.1 3.1 copy-start.13
  67.1 4.2 copy-start.12
  73.3 6.0 %copy-start.11 = (bf16[4,4,4,4,256]{4,3,2,1,0:T(4,128)(2,1)S(1)}, bf16[4,4,4,4,256]{4,3,2,1,0:T(4,128)(2,1)}, u32[]{:S(2)}) copy-start(bf16[4,4,4,4,256]{4,3,2,1,0:T(4,128)(2,1)} %get-tuple-element.166) | copy-start | bytes 393220
  75.4 7.5 %copy-start.3 = (bf16[3,256,256]{2,1,0:T(8,128)(2,1)S(1)}, bf16[3,256,256]{2,1,0:T(8,128)(2,1)}, u32[]{:S(2)}) copy-start(bf16[3,256,256]{2,1,0:T(8,128)(2,1)} %get-tuple-element.121) | copy-start | bytes 1179652
  82.9 2.7 copy-start.4
  82.9 3.0 copy-start.5
  84.2 1.9 copy-start.6
  85.6 1.0 copy-start.7
  85.9 1.0 copy-start.8
  86.2 1.1 copy-start.9
  86.6 1.0 copy-start.15
  86.6 1.1 copy-start.16
  87.7 1.3 copy-start.31
  106.2 10.0 %copy-start.24 = (s32[1,4,4]{2,1,0:T(4,128)S(1)}, s32[1,4,4]{2,1,0:T(4,128)}, u32[]{:S(2)}) copy-start(s32[1,4,4]{2,1,0:T(4,128)} %param.28) | copy-start | bytes 196
  106.2 103.3 %all-to-all-start.1 = ((bf16[32,2,32768]{2,1,0:T(2,128)(2,1)}), bf16[32,2,32768]{2,1,0:T(2,128)(2,1)}, u32[]{:S(2)}, u32[]{:S(2)}) async-start(bf16[32,2,32768]{2,1,0:T(2,128)(2,1)} %reshape.698), calls=%async_computation.1 | async-start | bytes 8388608 | tf_op jit(solution)/shard_map/all_to_all | solution.py:133
  116.2 426.1 %all-reduce.4.cloned.1.call-start = ((), (), s32[]{:S(2)}) async-start(), calls=%async_computation.2 | async-start | bytes 3538944 | tf_op jit(solution)/shard_map/psum | solution.py:166
  237.5 1.0 copy-start.14
  237.5 7.6 %copy-start.25 = (s32[4,4]{1,0:T(4,128)S(1)}, s32[4,4]{1,0:T(4,128)}, u32[]{:S(2)}) copy-start(s32[4,4]{1,0:T(4,128)} %get-tuple-element.204) | copy-start | bytes 196
  237.5 8.4 %copy-start.10 = (bf16[27,128,128]{2,1,0:T(8,128)(2,1)S(1)}, bf16[27,128,128]{2,1,0:T(8,128)(2,1)}, u32[]{:S(2)}) copy-start(bf16[27,128,128]{2,1,0:T(8,128)(2,1)} %param.33) | copy-start | bytes 2654212
  238.8 10.5 %collective-permute-start.3 = (bf16[4,4,8,8,128]{4,3,2,0,1:T(8,128)(2,1)S(1)}, bf16[4,4,8,8,128]{4,3,2,0,1:T(8,128)(2,1)S(1)}, u32[]{:S(2)}, u32[]{:S(2)}) collective-permute-start(bf16[4,4,8,8,128]{4,3,2,0,1:T(8,128)(2,1)S(1)} %pad_maximum_fusion.20), channel_id=1, source_target_pairs={{1,0},{2,1},{3,2},{4,3},{5,4},{6,5},{7,6},{8,7},{9,8},{10,9},{11,1... | collective-permute-start | bytes 786440 | tf_op jit(solution)/shard_map/ppermute | solution.py:20
  243.2 12.0 %collective-permute-start.2 = (bf16[4,4,8,8,128]{4,3,2,0,1:T(8,128)(2,1)S(1)}, bf16[4,4,8,8,128]{4,3,2,0,1:T(8,128)(2,1)S(1)}, u32[]{:S(2)}, u32[]{:S(2)}) collective-permute-start(bf16[4,4,8,8,128]{4,3,2,0,1:T(8,128)(2,1)S(1)} %pad_maximum_fusion.20), channel_id=1, source_target_pairs={{0,1},{1,2},{2,3},{3,4},{4,5},{5,6},{6,7},{7,8},{8,9},{9,10},{10,1... | collective-permute-start | bytes 786440 | tf_op jit(solution)/shard_map/ppermute | solution.py:18
  247.1 8.4 %copy-start.29 = (pred[4]{0:T(512)(128)(4,1)S(1)}, pred[4]{0:T(512)(128)(4,1)}, u32[]{:S(2)}) copy-start(pred[4]{0:T(512)(128)(4,1)} %get-tuple-element.101) | copy-start | bytes 16
  255.2 1.3 copy-start.28
  255.2 2.4 copy-start.27
  255.3 3.3 copy-start.26
  270.8 0.9 copy-start.21
  270.9 1.1 copy-start.33
  282.5 261.3 %copy-start.1 = (bf16[256,128]{1,0:T(8,128)(2,1)S(1)}, bf16[256,128]{1,0:T(8,128)(2,1)}, u32[]{:S(2)}) copy-start(bf16[256,128]{1,0:T(8,128)(2,1)} %param.32) | copy-start | bytes 196612
  283.2 1.2 copy-start.2
Sparse Core Ops, SparseCore 0:
  284.5 257.7 all-reduce.3
where the time goes:
time: 556 us; the launch traced here: 551 us
  waiting for transfers between devices  358 us (64%)
  local copies, waits for them, and re-layouts  72.8 us (13%)
  matrix products  41.5 us (7%)
  starting transfers between devices  34.6 us (6%)
  other arithmetic  28.9 us (5%)
  between operations  15.3 us (3%)
    psum x1, waiting for transfers between devices, body(): summed = lax.psum(running, ('scene', 'blk'))  258 us
    all_to_all x1, waiting for transfers between devices, body(): lax.all_to_all(packed, 'blk', split_axis=0, concat_axis=0, tiled=True)  91.8 us
    unnamed x77, local copies, waits for them, and re-layouts  31.3 us
    concatenate x18, other arithmetic, convolve(): jnp.concatenate([padded[:, off_x:off_x + side_cells, off_y:off_y + side_c...  13.2 us
    ppermute x2, starting transfers between devices, with_halo(): lax.ppermute(head, axis, [((i + 1) % count, i) for i in range(ends)])  12.1 us
  transfers between devices with their start and end apart: 7, of which 4 were waited for; matrix products, arithmetic and copies ran while one was open for 15% of the time, Pallas kernels for 0%

commit v1 on v0

--- a/solution.py
+++ b/solution.py
@@ -163,7 +163,7 @@
                     )
                 )
     running = jnp.stack(tap_terms, axis=1)
-    summed = lax.psum(running, ("scene", "blk"))
+    summed = lax.psum(lax.psum(running, "scene"), "blk")
     gradient = lax.dynamic_slice_in_dim(summed, position * shard_rows, shard_rows, 0)
     return (fine_out, gradient)
 

time: 556 us -> 520 us (0.935)
  waiting for transfers between devices: 358 us -> 321 us
    psum x1 -> x2, waiting for transfers between devices: 258 us -> 221 us  [body(): summed = lax.psum(lax.psum(running, 'scene'), 'blk')]
  transfers between devices with their start and end apart: 7 -> 8, of which waited for: 4 -> 5; matrix products, arithmetic and copies ran while one was open for 15% -> 16% of each run, Pallas kernels for 0% -> 0%
where the time goes in v1:
time: 520 us; the launch traced here: 514 us
  waiting for transfers between devices  321 us (62%)
  local copies, waits for them, and re-layouts  72.8 us (14%)
  matrix products  41.4 us (8%)
  starting transfers between devices  34.7 us (7%)
  other arithmetic  28.9 us (6%)
  between operations  15.3 us (3%)
    psum x2, waiting for transfers between devices, body(): summed = lax.psum(lax.psum(running, 'scene'), 'blk')  221 us
    all_to_all x1, waiting for transfers between devices, body(): lax.all_to_all(packed, 'blk', split_axis=0, concat_axis=0, tiled=True)  91.8 us
    unnamed x77, local copies, waits for them, and re-layouts  31.3 us
    concatenate x18, other arithmetic, convolve(): jnp.concatenate([padded[:, off_x:off_x + side_cells, off_y:off_y + side_c...  13.2 us
    ppermute x2, starting transfers between devices, with_halo(): lax.ppermute(head, axis, [((i + 1) % count, i) for i in range(ends)])  12.1 us
    dot_general x17, matrix products, convolve(): jnp.dot(stacked, weight[first_tap:first_tap + 3].reshape(3 * channels, -1...  10.6 us
  transfers between devices with their start and end apart: 8, of which 5 were waited for; matrix products, arithmetic and copies ran while one was open for 16% of the time, Pallas kernels for 0%

profile of v1, /device:TPU:2, one launch (start us, length us, event | category | flops | bytes accessed | tf_op | source)
XLA Modules:
  0.0 514.0 jit_solution(5570138872085383071)
XLA Ops:
  7.2 1.0 reshape_squeeze.28
  9.6 7.7 %collective-permute-start.1 = (bf16[4,4,4,4,256]{4,3,2,0,1:T(4,128)(2,1)}, bf16[4,4,4,4,256]{4,3,2,0,1:T(4,128)(2,1)}, u32[]{:S(2)}, u32[]{:S(2)}) collective-permute-start(bf16[4,4,4,4,256]{4,3,2,0,1:T(4,128)(2,1)} %pad_maximum_fusion.21), channel_id=1, source_target_pairs={{1,0},{2,1},{3,2},{4,3},{5,4},{6,5},{7,6},{8,7},{9,8},{10,9},{11,1... | collective-permute-start | bytes 393224 | tf_op jit(solution)/shard_map/ppermute | solution.py:20
  17.3 1.9 collective-permute-start
  23.4 8.6 %all-to-all-start = ((s32[32,1,1]{2,1,0:T(1,128)}), s32[32,1,1]{2,1,0:T(1,128)S(1)}, u32[]{:S(2)}, u32[]{:S(2)}) async-start(s32[32,1,1]{2,1,0:T(1,128)} %copy.71), calls=%async_computation | async-start | bytes 32768 | tf_op jit(solution)/shard_map/all_to_all | solution.py:134
  32.0 3.1 fusion.88
  36.5 1.6 fusion.53
  38.2 1.4 pad_maximum_fusion.10
  39.6 0.8 fusion.95
  40.4 1.6 reshape_squeeze.29
  42.0 1.7 convolution_convert_fusion.9
  44.5 1.6 reshape_squeeze.30
  46.1 1.7 convolution_convert_fusion.8
  47.8 1.4 reshape.606
  49.3 1.6 reshape_squeeze.31
  50.8 1.7 convolution_convert_fusion.7
  52.6 1.4 reshape.607
  54.7 1.1 convolution_convert_fusion.6
  56.1 0.9 scatter.29
  57.0 0.9 scatter.30
  58.6 1.1 fusion.94
  59.8 2.3 fusion.93
  62.3 0.8 reshape.609
  63.1 1.2 pad_maximum_fusion.12
  64.3 0.8 reshape.611
  65.1 1.1 pad_maximum_fusion.13
  66.3 0.9 reshape.613
  67.2 1.2 pad_maximum_fusion.14
  68.4 0.8 reshape.615
  69.2 1.2 pad_maximum_fusion.15
  70.4 0.9 reshape.617
  71.3 1.1 pad_maximum_fusion.16
  72.5 0.8 reshape.619
  73.3 1.2 pad_maximum_fusion.17
  74.5 0.9 reshape.621
  75.4 2.0 pad_maximum_fusion.18
  77.4 1.8 reshape.623
  79.3 1.8 pad_maximum_fusion.19
  81.1 1.8 reshape.625
  82.9 1.3 fusion.96
  84.3 1.3 convolution_add_fusion.15
  89.0 3.3 fusion
  92.9 6.8 %reduce.49 = bf16[32,65536]{1,0:T(8,128)(2,1)} reduce(bf16[32,1,65536]{2,0,1:T(8,128)(2,1)} %fusion, bf16[]{:T(256)} %broadcast.212), dimensions={1}, to_apply=%copy.79.reduce_sub_computation | reduce | bytes 8388610 | tf_op jit(solution)/shard_map/all_to_all | solution.py:133
  99.7 6.6 %reshape.698 = bf16[32,2,32768]{2,1,0:T(2,128)(2,1)} reshape(bf16[32,65536]{1,0:T(8,128)(2,1)} %reduce.49) | data formatting | bytes 8388608
  106.2 10.0 %all-to-all-start.1 = ((bf16[32,2,32768]{2,1,0:T(2,128)(2,1)}), bf16[32,2,32768]{2,1,0:T(2,128)(2,1)}, u32[]{:S(2)}, u32[]{:S(2)}) async-start(bf16[32,2,32768]{2,1,0:T(2,128)(2,1)} %reshape.698), calls=%async_computation.1 | async-start | bytes 8388608 | tf_op jit(solution)/shard_map/all_to_all | solution.py:133
  117.7 91.8 %all-to-all-done.1 = bf16[32,2,32768]{2,1,0:T(2,128)(2,1)} async-done(((bf16[32,2,32768]{2,1,0:T(2,128)(2,1)}), bf16[32,2,32768]{2,1,0:T(2,128)(2,1)}, u32[]{:S(2)}, u32[]{:S(2)}) %all-to-all-start.1) | async-done | bytes 4194336 | tf_op jit(solution)/shard_map/all_to_all | solution.py:133
  209.5 20.0 %reshape.699 = bf16[32,1,65536]{2,1,0:T(2,128)(2,1)} reshape(bf16[32,2,32768]{2,1,0:T(2,128)(2,1)} %all-to-all-done.1) | data formatting | bytes 8388608
  229.5 7.9 %fusion.4 = f32[1,4,512,128]{3,1,2,0:T(4,128)S(1)} fusion(bf16[32,1,65536]{2,1,0:T(2,128)(2,1)} %reshape.699, s32[32]{0:T(128)S(1)} %reduce.16, s32[4]{0:T(128)S(1)} %iota_add_fusion), kind=kOutput, calls=%fused_computation.31 | convolution fusion | flops 17301632 | bytes 5243024 | tf_op jit(solution)/shard_map/dot_general | solution.py:136
  237.6 0.9 copy-done.14
  238.8 4.4 collective-permute-start.3
  243.2 2.0 collective-permute-start.2
  245.2 0.8 slice_reduce_fusion
  247.1 2.2 collective-permute-done.3
  249.3 5.8 %collective-permute-done.2 = bf16[4,4,8,8,128]{4,3,2,0,1:T(8,128)(2,1)S(1)} collective-permute-done((bf16[4,4,8,8,128]{4,3,2,0,1:T(8,128)(2,1)S(1)}, bf16[4,4,8,8,128]{4,3,2,0,1:T(8,128)(2,1)S(1)}, u32[]{:S(2)}, u32[]{:S(2)}) %collective-permute-start.2) | collective-permute-done | bytes 262176 | tf_op jit(solution)/shard_map/ppermute | solution.py:18
  255.5 0.9 fusion.7
  256.6 0.9 fusion.8
  257.6 0.8 fusion.9
  258.6 0.9 fusion.10
  260.5 0.9 fusion.90
  261.4 2.8 fusion.89
  271.9 1.7 fusion.38
  283.2 1.2 copy-done.2
  284.4 67.0 %all-reduce.5.cloned.1.call-done = f32[128,27,128]{2,0,1:T(8,128)} async-done(((f32[128,27,128]{2,0,1:T(8,128)}), f32[128,27,128]{2,0,1:T(8,128)}) %all-reduce.5.cloned.1.call-update) | async-done | bytes 1769488 | tf_op jit(solution)/shard_map/psum | solution.py:166
  351.4 153.9 %all-reduce.7.cloned.1.call-done = f32[128,27,128]{2,0,1:T(8,128)} async-done(((f32[128,27,128]{2,0,1:T(8,128)}), f32[128,27,128]{2,0,1:T(8,128)}) %all-reduce.7.cloned.1.call-update) | async-done | bytes 1769488 | tf_op jit(solution)/shard_map/psum | solution.py:166
  505.3 1.5 constant_dynamic-slice_fusion
  (171 shorter events, 35.0 us)
Async XLA Ops:
  7.2 80.4 %copy-start = (bf16[256,128]{1,0:T(8,128)(2,1)S(1)}, bf16[256,128]{1,0:T(8,128)(2,1)}, u32[]{:S(2)}) copy-start(bf16[256,128]{1,0:T(8,128)(2,1)} %param.32) | copy-start | bytes 196612
  8.2 0.6 copy-start.17
  8.2 1.4 copy-start.18
  8.2 9.1 %copy-start.19 = (bf16[4,1,4,4,256]{4,3,2,0,1:T(4,128)(2,1)}, bf16[4,1,4,4,256]{4,3,2,0,1:T(4,128)(2,1)S(1)}, u32[]{:S(2)}) copy-start(bf16[4,1,4,4,256]{4,3,2,0,1:T(4,128)(2,1)S(1)} %get-tuple-element.200) | copy-start | bytes 98308
  8.3 11.0 %copy-start.20 = (bf16[4,1,4,4,256]{4,3,2,0,1:T(4,128)(2,1)}, bf16[4,1,4,4,256]{4,3,2,0,1:T(4,128)(2,1)S(1)}, u32[]{:S(2)}) copy-start(bf16[4,1,4,4,256]{4,3,2,0,1:T(4,128)(2,1)S(1)} %get-tuple-element.201) | copy-start | bytes 98308
  9.6 28.6 %collective-permute-start.1 = (bf16[4,4,4,4,256]{4,3,2,0,1:T(4,128)(2,1)}, bf16[4,4,4,4,256]{4,3,2,0,1:T(4,128)(2,1)}, u32[]{:S(2)}, u32[]{:S(2)}) collective-permute-start(bf16[4,4,4,4,256]{4,3,2,0,1:T(4,128)(2,1)} %pad_maximum_fusion.21), channel_id=1, source_target_pairs={{1,0},{2,1},{3,2},{4,3},{5,4},{6,5},{7,6},{8,7},{9,8},{10,9},{11,1... | collective-permute-start | bytes 393224 | tf_op jit(solution)/shard_map/ppermute | solution.py:20
  17.3 20.9 %collective-permute-start = (bf16[4,4,4,4,256]{4,3,2,0,1:T(4,128)(2,1)}, bf16[4,4,4,4,256]{4,3,2,0,1:T(4,128)(2,1)}, u32[]{:S(2)}, u32[]{:S(2)}) collective-permute-start(bf16[4,4,4,4,256]{4,3,2,0,1:T(4,128)(2,1)} %pad_maximum_fusion.21), channel_id=1, source_target_pairs={{0,1},{1,2},{2,3},{3,4},{4,5},{5,6},{6,7},{7,8},{8,9},{9,10},{10,1... | collective-permute-start | bytes 393224 | tf_op jit(solution)/shard_map/ppermute | solution.py:18
  21.3 0.6 copy-start.30
  23.4 82.9 %all-to-all-start = ((s32[32,1,1]{2,1,0:T(1,128)}), s32[32,1,1]{2,1,0:T(1,128)S(1)}, u32[]{:S(2)}, u32[]{:S(2)}) async-start(s32[32,1,1]{2,1,0:T(1,128)} %copy.71), calls=%async_computation | async-start | bytes 32768 | tf_op jit(solution)/shard_map/all_to_all | solution.py:134
  32.0 3.1 copy-start.22
  32.0 3.1 copy-start.23
  36.5 5.5 %copy-start.32 = (s32[4]{0:T(128)S(1)}, s32[4]{0:T(128)}, u32[]{:S(2)}) copy-start(s32[4]{0:T(128)} %get-tuple-element.113) | copy-start | bytes 52
  62.1 3.1 copy-start.13
  67.1 4.2 copy-start.12
  73.3 6.0 %copy-start.11 = (bf16[4,4,4,4,256]{4,3,2,1,0:T(4,128)(2,1)S(1)}, bf16[4,4,4,4,256]{4,3,2,1,0:T(4,128)(2,1)}, u32[]{:S(2)}) copy-start(bf16[4,4,4,4,256]{4,3,2,1,0:T(4,128)(2,1)} %get-tuple-element.166) | copy-start | bytes 393220
  75.4 7.5 %copy-start.3 = (bf16[3,256,256]{2,1,0:T(8,128)(2,1)S(1)}, bf16[3,256,256]{2,1,0:T(8,128)(2,1)}, u32[]{:S(2)}) copy-start(bf16[3,256,256]{2,1,0:T(8,128)(2,1)} %get-tuple-element.121) | copy-start | bytes 1179652
  82.9 2.7 copy-start.4
  82.9 3.0 copy-start.5
  84.2 1.9 copy-start.6
  85.6 1.0 copy-start.7
  85.9 1.0 copy-start.8
  86.2 1.1 copy-start.9
  86.6 1.0 copy-start.15
  86.6 1.1 copy-start.16
  87.7 1.3 copy-start.31
  106.2 10.0 %copy-start.24 = (s32[1,4,4]{2,1,0:T(4,128)S(1)}, s32[1,4,4]{2,1,0:T(4,128)}, u32[]{:S(2)}) copy-start(s32[1,4,4]{2,1,0:T(4,128)} %param.28) | copy-start | bytes 196
  106.2 103.3 %all-to-all-start.1 = ((bf16[32,2,32768]{2,1,0:T(2,128)(2,1)}), bf16[32,2,32768]{2,1,0:T(2,128)(2,1)}, u32[]{:S(2)}, u32[]{:S(2)}) async-start(bf16[32,2,32768]{2,1,0:T(2,128)(2,1)} %reshape.698), calls=%async_computation.1 | async-start | bytes 8388608 | tf_op jit(solution)/shard_map/all_to_all | solution.py:133
  116.2 235.2 %all-reduce.5.cloned.1.call-start = ((), (), s32[]{:S(2)}) async-start(), calls=%async_computation.2 | async-start | bytes 3538944 | tf_op jit(solution)/shard_map/psum | solution.py:166
  237.5 1.0 copy-start.14
  237.5 7.6 %copy-start.25 = (s32[4,4]{1,0:T(4,128)S(1)}, s32[4,4]{1,0:T(4,128)}, u32[]{:S(2)}) copy-start(s32[4,4]{1,0:T(4,128)} %get-tuple-element.204) | copy-start | bytes 196
  237.5 8.4 %copy-start.10 = (bf16[27,128,128]{2,1,0:T(8,128)(2,1)S(1)}, bf16[27,128,128]{2,1,0:T(8,128)(2,1)}, u32[]{:S(2)}) copy-start(bf16[27,128,128]{2,1,0:T(8,128)(2,1)} %param.33) | copy-start | bytes 2654212
  238.8 10.5 %collective-permute-start.3 = (bf16[4,4,8,8,128]{4,3,2,0,1:T(8,128)(2,1)S(1)}, bf16[4,4,8,8,128]{4,3,2,0,1:T(8,128)(2,1)S(1)}, u32[]{:S(2)}, u32[]{:S(2)}) collective-permute-start(bf16[4,4,8,8,128]{4,3,2,0,1:T(8,128)(2,1)S(1)} %pad_maximum_fusion.20), channel_id=1, source_target_pairs={{1,0},{2,1},{3,2},{4,3},{5,4},{6,5},{7,6},{8,7},{9,8},{10,9},{11,1... | collective-permute-start | bytes 786440 | tf_op jit(solution)/shard_map/ppermute | solution.py:20
  243.2 12.0 %collective-permute-start.2 = (bf16[4,4,8,8,128]{4,3,2,0,1:T(8,128)(2,1)S(1)}, bf16[4,4,8,8,128]{4,3,2,0,1:T(8,128)(2,1)S(1)}, u32[]{:S(2)}, u32[]{:S(2)}) collective-permute-start(bf16[4,4,8,8,128]{4,3,2,0,1:T(8,128)(2,1)S(1)} %pad_maximum_fusion.20), channel_id=1, source_target_pairs={{0,1},{1,2},{2,3},{3,4},{4,5},{5,6},{6,7},{7,8},{8,9},{9,10},{10,1... | collective-permute-start | bytes 786440 | tf_op jit(solution)/shard_map/ppermute | solution.py:18
  247.1 8.4 %copy-start.29 = (pred[4]{0:T(512)(128)(4,1)S(1)}, pred[4]{0:T(512)(128)(4,1)}, u32[]{:S(2)}) copy-start(pred[4]{0:T(512)(128)(4,1)} %get-tuple-element.101) | copy-start | bytes 16
  255.2 1.3 copy-start.28
  255.2 2.4 copy-start.27
  255.3 3.3 copy-start.26
  270.8 0.9 copy-start.21
  270.9 1.1 copy-start.33
  283.2 1.2 copy-start.2
  283.2 223.7 %copy-start.1 = (bf16[256,128]{1,0:T(8,128)(2,1)S(1)}, bf16[256,128]{1,0:T(8,128)(2,1)}, u32[]{:S(2)}) copy-start(bf16[256,128]{1,0:T(8,128)(2,1)} %param.32) | copy-start | bytes 196612
  284.4 220.9 %all-reduce.7.cloned.1.call-start = ((), (), s32[]{:S(2)}) async-start(), calls=%async_computation.3 | async-start | bytes 3538944 | tf_op jit(solution)/shard_map/psum | solution.py:166
Sparse Core Ops, SparseCore 0:
  284.5 66.8 all-reduce.4
  354.9 150.4 all-reduce.6
